TPU v7x, 32 devices: a whole 2x2x4 slice. The times are simulated.
32 devices in a mesh: dp: 8 (over z, y), tensor: 4 (over x, core).
Axes of the slice: x: 2, y: 2, z: 4, core: 2. Of those that a mesh axis runs over, the one named last changes fastest.
Arguments:
- layer_input: bfloat16 [4096, 1024], P(('dp', 'tensor')), may hold values from -6 to 6
- segments: int32 [4096], P('dp'), may hold values from 0 to 23, as said below
- positions: int32 [4096], P('dp'), may hold values from 0 to 1535, as said below
- first_gain: float32 [1024], replicated, may hold values from 0.5 to 1.5
- merged_weight: bfloat16 [1024, 3, 1024], P('dp', None, 'tensor'), may hold values from -0.1875 to 0.1875
- output_weight: bfloat16 [1024, 1024], P('tensor', 'dp'), may hold values from -1 to 1
- second_gain: float32 [1024], replicated, may hold values from 0.5 to 1.5
- expand_weight: bfloat16 [1024, 2, 2624], P('dp', None, 'tensor'), may hold values from -0.1875 to 0.1875
- shrink_weight: bfloat16 [2624, 1024], P('tensor', 'dp'), may hold values from -0.125 to 0.125
- cotangent: bfloat16 [4096, 1024], P(('dp', 'tensor')), may hold values from -6 to 6
Outputs:
- layer_output: bfloat16 [4096, 1024], P(('dp', 'tensor'))
- input_grad: float32 [4096, 1024], P(('dp', 'tensor'))
- first_gain_grad: float32 [1024], replicated
- merged_grad: float32 [1024, 3, 1024], P('dp', None, 'tensor')
- output_grad: float32 [1024, 1024], P('tensor', 'dp')
- second_gain_grad: float32 [1024], replicated
- expand_grad: float32 [1024, 2, 2624], P('dp', None, 'tensor')
- shrink_grad: float32 [2624, 1024], P('tensor', 'dp')
Inputs may be any that keep to these rules, and one draw needn't show every extreme that they name: `segments`: numbers never fall along the tokens; the block of 512 tokens with index g holds the numbers 3 g, 3 g + 1 and 3 g + 2, each on one token or more. Within a document the positions rise by one from token to token.
All inputs are finite; a program needn't handle non-finite values.
Results may differ from a plain program's by a relative error of at most 0.018.
Values may be sent and summed in bfloat16 or wider, within the bound.
A program may use at most 128 MiB of HBM per device.

v0:
```python
from functools import partial

import jax
import jax.numpy as jnp
from jax import lax
from jax.sharding import PartitionSpec as P

WINDOW = 128
HEAD_DIM = 64


epsilon = 1e-05
rope_base = 10000.0
masked_score = -1e30


def layer_norm(layer_rows, gain):
    center = layer_rows - jnp.mean(layer_rows, axis=-1, keepdims=True)
    inverse = lax.rsqrt(jnp.mean(center * center, axis=-1, keepdims=True) + epsilon)
    normal_rows = center * inverse
    return (normal_rows * gain, normal_rows, inverse)


def norm_back(grad_normed, normal_rows, inverse, gain):
    grad_hat = grad_normed * gain
    gain_term = jnp.sum(grad_normed * normal_rows, axis=0)
    mean_grad = jnp.mean(grad_hat, axis=-1, keepdims=True)
    mean_cross = jnp.mean(grad_hat * normal_rows, axis=-1, keepdims=True)
    return ((grad_hat - mean_grad - normal_rows * mean_cross) * inverse, gain_term)


def rope_tables(positions):
    half_dim = HEAD_DIM // 2
    frequency = rope_base ** (-2.0 * jnp.arange(half_dim, dtype=jnp.float32) / HEAD_DIM)
    angles = positions.astype(jnp.float32)[:, None] * frequency[None, :]
    return (jnp.cos(angles), jnp.sin(angles))


def rotate(head_rows, cosine_table, sine_table):
    half_dim = head_rows.shape[-1] // 2
    first_half = head_rows[..., :half_dim]
    second_half = head_rows[..., half_dim:]
    cosine_b = cosine_table[:, None, :]
    sine_b = sine_table[:, None, :]
    return jnp.concatenate(
        [
            first_half * cosine_b - second_half * sine_b,
            second_half * cosine_b + first_half * sine_b,
        ],
        axis=-1,
    )


def band_scores(query_blk, key_blk, segments, seg_pad, offset, block_rows):
    half_window = WINDOW // 2
    raw_scores = jnp.einsum("qhd,khd->hqk", query_blk, key_blk, preferred_element_type=jnp.float32)
    rows_at = offset + jnp.arange(block_rows, dtype=jnp.int32)
    cols_at = offset - half_window + jnp.arange(block_rows + WINDOW, dtype=jnp.int32)
    allowed = (segments[:, None] == seg_pad[None, :]) & (
        jnp.abs(rows_at[:, None] - cols_at[None, :]) <= half_window
    )
    return jnp.where(allowed[None], raw_scores * HEAD_DIM ** (-0.5), masked_score)


def padded_keys(keys_rot, value_rows, segments):
    half_window = WINDOW // 2
    pad_spec = ((half_window, half_window), (0, 0), (0, 0))
    seg_pad = jnp.pad(segments, (half_window, half_window), constant_values=-1)
    return (jnp.pad(keys_rot, pad_spec), jnp.pad(value_rows, pad_spec), seg_pad)


def band_forward(queries, keys_rot, value_rows, segments):
    group_size = queries.shape[0]
    block_rows = min(512, group_size)
    keys_pad, values_pad, seg_pad = padded_keys(keys_rot, value_rows, segments)

    def one_block(block_index):
        offset = block_index * block_rows
        scores = band_scores(queries, keys_pad, segments, seg_pad, offset, block_rows)
        row_max = jnp.max(scores, axis=-1, keepdims=True)
        weights = jnp.exp(scores - row_max)
        row_total = jnp.sum(weights, axis=-1, keepdims=True)
        softmax_out = (weights / row_total).astype(jnp.bfloat16)
        attended = jnp.einsum(
            "hqk,khd->qhd", softmax_out, values_pad, preferred_element_type=jnp.float32
        )
        return (attended, row_max[..., 0] + jnp.log(row_total[..., 0]))

    attended, log_total = lax.map(one_block, jnp.arange(group_size // block_rows, dtype=jnp.int32))
    return (attended.reshape(queries.shape), log_total)


def band_backward(queries, keys_rot, value_rows, segments, log_total, grad_attended):
    group_size = queries.shape[0]
    block_rows = min(512, group_size)
    half_window = WINDOW // 2
    keys_pad, values_pad, seg_pad = padded_keys(keys_rot, value_rows, segments)
    padded_shape = keys_pad.shape

    def one_step(carried, block_index):
        grad_keys, grad_values = carried
        offset = block_index * block_rows
        scores = band_scores(queries, keys_pad, segments, seg_pad, offset, block_rows)
        softmax_out = jnp.exp(scores - log_total[block_index][:, :, None])
        grad_value_blk = jnp.einsum(
            "hqk,qhd->khd",
            softmax_out.astype(jnp.bfloat16),
            grad_attended,
            preferred_element_type=jnp.float32,
        )
        grad_probs = jnp.einsum(
            "qhd,khd->hqk", grad_attended, values_pad, preferred_element_type=jnp.float32
        )
        inner = jnp.sum(grad_probs * softmax_out, axis=-1, keepdims=True)
        grad_raw = (softmax_out * (grad_probs - inner) * HEAD_DIM ** (-0.5)).astype(jnp.bfloat16)
        grad_query_blk = jnp.einsum(
            "hqk,khd->qhd", grad_raw, keys_pad, preferred_element_type=jnp.float32
        )
        grad_key_blk = jnp.einsum(
            "hqk,qhd->khd", grad_raw, queries, preferred_element_type=jnp.float32
        )
        grad_keys = grad_keys + grad_key_blk
        grad_values = grad_values + grad_value_blk
        return ((grad_keys, grad_values), grad_query_blk)

    zero_pad = jnp.zeros(padded_shape, jnp.float32)
    (grad_keys, grad_values), grad_queries = lax.scan(
        one_step, (zero_pad, zero_pad), jnp.arange(group_size // block_rows, dtype=jnp.int32)
    )
    return (
        grad_queries.reshape(queries.shape),
        grad_keys[half_window : half_window + group_size],
        grad_values[half_window : half_window + group_size],
    )


def local(
    layer_input,
    segments,
    positions,
    first_gain,
    merged_weight,
    output_weight,
    second_gain,
    expand_weight,
    shrink_weight,
    cotangent,
):
    head_cols = merged_weight.shape[2]
    heads_here = head_cols // HEAD_DIM
    merged_full, output_full = (
        lax.all_gather(merged_weight, "dp", axis=0, tiled=True),
        lax.all_gather(output_weight, "dp", axis=1, tiled=True),
    )
    layer_rows = layer_input.astype(jnp.float32)
    norm_one, hat_one, inverse_one = layer_norm(layer_rows, first_gain)
    normed = lax.all_gather(norm_one.astype(jnp.bfloat16), "tensor", axis=0, tiled=True)
    group_size = normed.shape[0]
    merged_rows = jnp.einsum("td,dcf->tcf", normed, merged_full, preferred_element_type=jnp.float32)
    cosine_table, sine_table = rope_tables(positions)
    queries = rotate(
        merged_rows[:, 0].reshape(group_size, heads_here, HEAD_DIM), cosine_table, sine_table
    ).astype(jnp.bfloat16)
    keys_rot = rotate(
        merged_rows[:, 1].reshape(group_size, heads_here, HEAD_DIM), cosine_table, sine_table
    ).astype(jnp.bfloat16)
    value_rows = merged_rows[:, 2].reshape(group_size, heads_here, HEAD_DIM).astype(jnp.bfloat16)
    attended, log_total = band_forward(queries, keys_rot, value_rows, segments)
    attended_low = attended.reshape(group_size, head_cols).astype(jnp.bfloat16)
    middle = layer_rows + lax.psum_scatter(
        jnp.dot(attended_low, output_full, preferred_element_type=jnp.float32),
        "tensor",
        scatter_dimension=0,
        tiled=True,
    )
    norm_two, hat_two, inverse_two = layer_norm(middle, second_gain)
    expand_full, shrink_full = (
        lax.all_gather(expand_weight, "dp", axis=0, tiled=True),
        lax.all_gather(shrink_weight, "dp", axis=1, tiled=True),
    )
    normed_two = lax.all_gather(norm_two.astype(jnp.bfloat16), "tensor", axis=0, tiled=True)
    gate_up = jnp.einsum("td,dcf->tcf", normed_two, expand_full, preferred_element_type=jnp.float32)
    activated = jax.nn.gelu(gate_up[:, 0], approximate=False)
    hidden = (activated * gate_up[:, 1]).astype(jnp.bfloat16)
    result = middle + lax.psum_scatter(
        jnp.dot(hidden, shrink_full, preferred_element_type=jnp.float32).astype(jnp.bfloat16),
        "tensor",
        scatter_dimension=0,
        tiled=True,
    ).astype(jnp.float32)
    layer_output = result.astype(jnp.bfloat16)
    grad_out = cotangent.astype(jnp.float32)
    expand_full, shrink_full = (
        lax.all_gather(expand_weight, "dp", axis=0, tiled=True),
        lax.all_gather(shrink_weight, "dp", axis=1, tiled=True),
    )
    grad_mlp = lax.all_gather(cotangent, "tensor", axis=0, tiled=True)
    grad_hidden = jnp.einsum("td,fd->tf", grad_mlp, shrink_full, preferred_element_type=jnp.float32)
    shrink_term = jnp.einsum("tf,td->fd", hidden, grad_mlp, preferred_element_type=jnp.float32)
    unused, gelu_back = jax.vjp(partial(jax.nn.gelu, approximate=False), gate_up[:, 0])
    grad_input_half = gelu_back(grad_hidden * gate_up[:, 1])[0]
    grad_gate_up = jnp.stack([grad_input_half, grad_hidden * activated], axis=1).astype(
        jnp.bfloat16
    )
    expand_term = jnp.einsum(
        "td,tcf->dcf", normed_two, grad_gate_up, preferred_element_type=jnp.float32
    )
    grad_norm_two = lax.psum_scatter(
        jnp.einsum(
            "tcf,dcf->td", grad_gate_up, expand_full, preferred_element_type=jnp.float32
        ).astype(jnp.bfloat16),
        "tensor",
        scatter_dimension=0,
        tiled=True,
    ).astype(jnp.float32)
    grad_back_two, gain_two_term = norm_back(grad_norm_two, hat_two, inverse_two, second_gain)
    grad_middle = grad_out + grad_back_two
    shrink_grad, expand_grad = (
        lax.psum_scatter(shrink_term, "dp", scatter_dimension=1, tiled=True),
        lax.psum_scatter(expand_term, "dp", scatter_dimension=0, tiled=True),
    )
    merged_full, output_full = (
        lax.all_gather(merged_weight, "dp", axis=0, tiled=True),
        lax.all_gather(output_weight, "dp", axis=1, tiled=True),
    )
    grad_branch = lax.all_gather(grad_middle.astype(jnp.bfloat16), "tensor", axis=0, tiled=True)
    grad_attended = jnp.einsum(
        "td,ed->te", grad_branch, output_full, preferred_element_type=jnp.float32
    ).astype(jnp.bfloat16)
    output_term = jnp.einsum(
        "te,td->ed", attended_low, grad_branch, preferred_element_type=jnp.float32
    )
    grad_queries, grad_keys, grad_values = band_backward(
        queries,
        keys_rot,
        value_rows,
        segments,
        log_total,
        grad_attended.reshape(group_size, heads_here, HEAD_DIM),
    )
    grad_queries = rotate(grad_queries, cosine_table, -sine_table).reshape(group_size, head_cols)
    grad_keys = rotate(grad_keys, cosine_table, -sine_table).reshape(group_size, head_cols)
    grad_merged = jnp.stack(
        [grad_queries, grad_keys, grad_values.reshape(group_size, head_cols)], axis=1
    ).astype(jnp.bfloat16)
    merged_term = jnp.einsum("td,tcf->dcf", normed, grad_merged, preferred_element_type=jnp.float32)
    grad_norm_one = lax.psum_scatter(
        jnp.einsum(
            "tcf,dcf->td", grad_merged, merged_full, preferred_element_type=jnp.float32
        ).astype(jnp.bfloat16),
        "tensor",
        scatter_dimension=0,
        tiled=True,
    ).astype(jnp.float32)
    grad_back_one, gain_one_term = norm_back(grad_norm_one, hat_one, inverse_one, first_gain)
    input_grad = grad_middle + grad_back_one
    merged_grad, output_grad = (
        lax.psum_scatter(merged_term, "dp", scatter_dimension=0, tiled=True),
        lax.psum_scatter(output_term, "dp", scatter_dimension=1, tiled=True),
    )
    first_gain_grad, second_gain_grad = lax.psum((gain_one_term, gain_two_term), ("dp", "tensor"))
    return (
        layer_output,
        input_grad,
        first_gain_grad,
        merged_grad,
        output_grad,
        second_gain_grad,
        expand_grad,
        shrink_grad,
    )


def solution(mesh):
    placed = (
        P(("dp", "tensor"), None),
        P("dp"),
        P("dp"),
        P(),
        P("dp", None, "tensor"),
        P("tensor", "dp"),
        P(),
        P("dp", None, "tensor"),
        P("tensor", "dp"),
        P(("dp", "tensor"), None),
    )
    return jax.shard_map(
        local,
        mesh=mesh,
        in_specs=placed,
        out_specs=(
            P(("dp", "tensor"), None),
            P(("dp", "tensor"), None),
            P(),
            P("dp", None, "tensor"),
            P("tensor", "dp"),
            P(),
            P("dp", None, "tensor"),
            P("tensor", "dp"),
        ),
        check_vma=False,
    )
```

profile of v0, /device:TPU:0, one launch (start us, length us, event | category | flops | bytes accessed | tf_op | source)
XLA Modules:
  0.0 752.6 jit_solution(14217446691598072401)
XLA Ops:
  7.3 1.1 convert_reduce_fusion
  8.4 1.2 fusion.81
  10.1 1.9 fusion.77
  13.4 29.5 %all_gather.30 = bf16[256,1024]{1,0:T(8,128)(2,1)S(1)} all-gather(bf16[256,128]{1,0:T(8,128)(2,1)S(1)} %copy-done.24), channel_id=1, replica_groups=mesh['dp'=8,'tensor'=4] {'dp'}, dimensions={1}, use_global_device_ids=true | all-gather | bytes 589824 | tf_op jit(solution)/shard_map/all_gather | solution.py:153
  43.4 36.1 %all-gather.10.cloned.1.call-done = bf16[1024,3,256]{0,2,1:T(8,128)(2,1)} async-done(((bf16[128,3,256]{0,2,1:T(8,128)(2,1)}), bf16[1024,3,256]{0,2,1:T(8,128)(2,1)}) %all-gather.10.cloned.1.call-update) | async-done | bytes 1572880 | tf_op jit(solution)/shard_map/all_gather | solution.py:152
  79.5 2.7 fusion.62
  82.6 1.4 fusion.115
  84.1 1.3 fusion.2
  85.4 1.1 copy-done
  86.5 1.7 fusion.52
  88.9 1.8 fusion.116
  92.5 28.0 %reduce-scatter.9.cloned.1.call-done = f32[128,1024]{1,0:T(8,128)} async-done(((f32[512,1024]{1,0:T(8,128)}), f32[128,1024]{1,0:T(8,128)}) %reduce-scatter.9.cloned.1.call-update) | async-done | bytes 524304 | tf_op jit(solution)/shard_map/reduce_scatter | solution.py:170
  120.4 1.2 fusion.113
  121.8 0.8 multiply_convert_fusion.3
  122.9 15.8 %all-gather.18.cloned.1.call-done = bf16[512,1024]{1,0:T(8,128)(2,1)} async-done(((bf16[128,1024]{1,0:T(8,128)(2,1)}), bf16[512,1024]{1,0:T(8,128)(2,1)}) %all-gather.18.cloned.1.call-update) | async-done | bytes 1048592 | tf_op jit(solution)/shard_map/all_gather | solution.py:197
  138.7 44.7 %all-gather.16.cloned.1.call-done = bf16[656,1024]{1,0:T(8,128)(2,1)} async-done(((bf16[656,128]{1,0:T(8,128)(2,1)}), bf16[656,1024]{1,0:T(8,128)(2,1)}) %all-gather.16.cloned.1.call-update) | async-done | bytes 1343504 | tf_op jit(solution)/shard_map/all_gather | solution.py:179
  183.4 2.5 fusion.117
  186.0 55.8 %all-gather.14.cloned.1.call-done = bf16[1024,2,656]{0,2,1:T(8,128)(2,1)} async-done(((bf16[128,2,656]{0,2,1:T(8,128)(2,1)}), bf16[1024,2,656]{0,2,1:T(8,128)(2,1)}) %all-gather.14.cloned.1.call-update) | async-done | bytes 2686992 | tf_op jit(solution)/shard_map/all_gather | solution.py:178
  241.8 17.1 %all-gather.12.cloned.1.call-done = bf16[512,1024]{1,0:T(8,128)(2,1)} async-done(((bf16[128,1024]{1,0:T(8,128)(2,1)}), bf16[512,1024]{1,0:T(8,128)(2,1)}) %all-gather.12.cloned.1.call-update) | async-done | bytes 1048592 | tf_op jit(solution)/shard_map/all_gather | solution.py:181
  259.0 3.7 fusion.58
  262.7 3.2 fusion.65
  268.2 2.8 bitcast_convert_fusion.1
  271.1 2.0 convolution_convert_fusion
  273.2 22.9 %reduce-scatter.13.cloned.1.call-done = bf16[128,1024]{1,0:T(8,128)(2,1)} async-done(((bf16[512,1024]{1,0:T(8,128)(2,1)}), bf16[128,1024]{1,0:T(8,128)(2,1)}) %reduce-scatter.13.cloned.1.call-update) | async-done | bytes 262160 | tf_op jit(solution)/shard_map/reduce_scatter | solution.py:208
  296.1 1.8 fusion.86
  297.9 25.6 %reduce-scatter.11.cloned.1.call-done = bf16[128,1024]{1,0:T(8,128)(2,1)} async-done(((bf16[512,1024]{1,0:T(8,128)(2,1)}), bf16[128,1024]{1,0:T(8,128)(2,1)}) %reduce-scatter.11.cloned.1.call-update) | async-done | bytes 262160 | tf_op jit(solution)/shard_map/reduce_scatter | solution.py:185
  323.6 2.0 fusion.110
  325.9 16.6 %all-gather.20.cloned.1.call-done = bf16[512,1024]{1,0:T(8,128)(2,1)} async-done(((bf16[128,1024]{1,0:T(8,128)(2,1)}), bf16[512,1024]{1,0:T(8,128)(2,1)}) %all-gather.20.cloned.1.call-update) | async-done | bytes 1048592 | tf_op jit(solution)/shard_map/all_gather | solution.py:226
  342.5 1.7 convolution_convert_fusion.1
  344.2 3.2 fusion.92
  347.4 3.5 fusion.53
  351.0 18.6 %fusion.46 = f32[512,4,64]{0,2,1:T(8,128)S(1)} fusion(f32[4,512,640]{2,1,0:T(8,128)} %fusion.92, f32[4,512,640]{2,1,0:T(8,128)} %copy-done, f32[4,512]{1,0:T(4,128)S(1)} %log_add_fusion, bf16[512,4,32]{0,2,1:T(8,128)(2,1)S(1)} %copy-done.23, bf16[512,4,32]{0,2,1:T(8,128)(2,1)S(1)} %copy-done.21), kind=kOutput, calls=%fused_computation.58 | convolution fusion | flops 178424448 | bytes 11280384 | tf_op jit(solution)/shard_map/while/body/eval_jaxpr/hqk,khd->qhd/dot_general | solution.py:116
  369.6 16.4 %fusion.43 = f32[640,4,64]{0,2,1:T(8,128)} fusion(f32[4,512,640]{2,1,0:T(8,128)} %fusion.92, f32[4,512,640]{2,1,0:T(8,128)} %copy-done, f32[4,512]{1,0:T(4,128)S(1)} %log_add_fusion, bf16[512,4,32]{0,2,1:T(8,128)(2,1)S(1)} %copy-done.17, bf16[512,4,32]{0,2,1:T(8,128)(2,1)S(1)} %copy-done.19), kind=kOutput, calls=%fused_computation.56 | convolution fusion | flops 177474176 | bytes 11411456 | tf_op jit(solution)/shard_map/while/body/eval_jaxpr/hqk,qhd->khd/dot_general | solution.py:119
  386.3 1.3 subtract_convert_fusion.1
  387.9 3.5 bitcast_convert_fusion
  391.5 2.4 fusion.119
  394.0 1.1 copy-done.4
  395.2 1.4 fusion.118
  396.7 3.9 fusion.60
  401.9 5.1 fusion.56
  407.0 9.5 %reduce-scatter.15.cloned.1.call-done = bf16[128,1024]{1,0:T(8,128)(2,1)} async-done(((bf16[512,1024]{1,0:T(8,128)(2,1)}), bf16[128,1024]{1,0:T(8,128)(2,1)}) %reduce-scatter.15.cloned.1.call-update) | async-done | bytes 262160 | tf_op jit(solution)/shard_map/reduce_scatter | solution.py:247
  416.5 1.2 fusion.88
  417.8 40.4 %all-reduce.3 = (f32[1024]{0:T(1024)}, f32[1024]{0:T(1024)}) all-reduce(f32[1024]{0:T(1024)S(1)} %get-tuple-element.56, f32[1024]{0:T(1024)S(1)} %copy-done.27), channel_id=1, replica_groups=mesh['dp'=8,'tensor'=4] {'dp','tensor'}, use_global_device_ids=true, to_apply=%region_16.17 | all-reduce | flops 2048 | bytes 16384 | tf_op jit(solution)/shard_map/psum | solution.py:261
  458.2 2.0 fusion.80
  460.2 32.9 %reduce-scatter.23.cloned.1.call-done = f32[656,128]{1,0:T(8,128)} async-done(((f32[656,1024]{1,0:T(8,128)}), f32[656,128]{1,0:T(8,128)}) %reduce-scatter.23.cloned.1.call-update) | async-done | bytes 335888 | tf_op jit(solution)/shard_map/reduce_scatter | solution.py:219
  493.1 66.9 %reduce-scatter.19.cloned.1.call-done = f32[256,128]{1,0:T(8,128)} async-done(((f32[256,1024]{1,0:T(8,128)}), f32[256,128]{1,0:T(8,128)}) %reduce-scatter.19.cloned.1.call-update) | async-done | bytes 131088 | tf_op jit(solution)/shard_map/reduce_scatter | solution.py:259
  560.0 78.1 %reduce-scatter.17.cloned.1.call-done = f32[128,3,256]{2,0,1:T(8,128)} async-done(((f32[1024,3,256]{2,0,1:T(8,128)}), f32[128,3,256]{2,0,1:T(8,128)}) %reduce-scatter.17.cloned.1.call-update) | async-done | bytes 393232 | tf_op jit(solution)/shard_map/reduce_scatter | solution.py:258
  638.1 108.0 %reduce-scatter.21.cloned.1.call-done = f32[128,2,656]{0,2,1:T(8,128)} async-done(((f32[1024,2,656]{0,2,1:T(8,128)}), f32[128,2,656]{0,2,1:T(8,128)}) %reduce-scatter.21.cloned.1.call-update) | async-done | bytes 671760 | tf_op jit(solution)/shard_map/reduce_scatter | solution.py:220
  (127 shorter events, 10.4 us)
Async XLA Ops:
  7.2 4.9 copy-start.15
  7.2 5.8 copy-start.33
  7.2 5.8 copy-start.28
  7.2 6.2 copy-start.24
  7.2 36.2 %all-gather.8.cloned.1.call-start = ((), (), s32[]{:S(2)}) async-start(), calls=%async_computation.8 | async-start | bytes 1310720 | tf_op jit(solution)/shard_map/all_gather | solution.py:157
  8.4 1.2 copy-start.29
  12.0 67.5 %all-gather.10.cloned.1.call-start = ((), (), s32[]{:S(2)}) async-start(), calls=%async_computation.9 | async-start | bytes 1769472 | tf_op jit(solution)/shard_map/all_gather | solution.py:152
  12.9 107.5 %reduce-scatter.9.cloned.1.call-start = ((), (), s32[]{:S(2)}) async-start(), calls=%async_computation.10 | async-start | bytes 2621440 | tf_op jit(solution)/shard_map/reduce_scatter | solution.py:170
  82.3 3.1 copy-start.2
  82.6 1.5 copy-start.16
  82.6 1.5 copy-start.18
  82.6 1.5 copy-start.20
  82.6 1.5 copy-start.22
  84.1 2.4 copy-start
  90.6 29.8 %copy-start.1 = (bf16[128,1024]{1,0:T(8,128)(2,1)S(1)}, bf16[128,1024]{1,0:T(8,128)(2,1)}, u32[]{:S(2)}) copy-start(bf16[128,1024]{1,0:T(8,128)(2,1)} %param.10) | copy-start | bytes 786436
  90.7 31.2 %copy-start.25 = (f32[1024]{0:T(1024)S(1)}, f32[1024]{0:T(1024)}, u32[]{:S(2)}) copy-start(f32[1024]{0:T(1024)} %param.16) | copy-start | bytes 12292
  90.7 48.0 %all-gather.18.cloned.1.call-start = ((), (), s32[]{:S(2)}) async-start(), calls=%async_computation.15 | async-start | bytes 1310720 | tf_op jit(solution)/shard_map/all_gather | solution.py:197
  91.3 92.2 %all-gather.16.cloned.1.call-start = ((), (), s32[]{:S(2)}) async-start(), calls=%async_computation.13 | async-start | bytes 1511424 | tf_op jit(solution)/shard_map/all_gather | solution.py:179
  91.9 150.0 %all-gather.14.cloned.1.call-start = ((), (), s32[]{:S(2)}) async-start(), calls=%async_computation.12 | async-start | bytes 3022848 | tf_op jit(solution)/shard_map/all_gather | solution.py:178
  92.4 166.5 %all-gather.12.cloned.1.call-start = ((), (), s32[]{:S(2)}) async-start(), calls=%async_computation.11 | async-start | bytes 1310720 | tf_op jit(solution)/shard_map/all_gather | solution.py:181
  122.7 173.4 %reduce-scatter.13.cloned.1.call-start = ((), (), s32[]{:S(2)}) async-start(), calls=%async_computation.16 | async-start | bytes 1310720 | tf_op jit(solution)/shard_map/reduce_scatter | solution.py:208
  265.9 0.9 copy-start.9
  265.9 2.2 copy-start.34
  268.2 2.9 copy-start.35
  271.1 52.5 %reduce-scatter.11.cloned.1.call-start = ((), (), s32[]{:S(2)}) async-start(), calls=%async_computation.14 | async-start | bytes 1310720 | tf_op jit(solution)/shard_map/reduce_scatter | solution.py:185
  273.1 50.4 %copy-start.7 = (bf16[128,1024]{1,0:T(8,128)(2,1)S(1)}, bf16[128,1024]{1,0:T(8,128)(2,1)}, u32[]{:S(2)}) copy-start(bf16[128,1024]{1,0:T(8,128)(2,1)} %param.19) | copy-start | bytes 786436
  273.1 69.3 %all-gather.20.cloned.1.call-start = ((), (), s32[]{:S(2)}) async-start(), calls=%async_computation.17 | async-start | bytes 1310720 | tf_op jit(solution)/shard_map/all_gather | solution.py:226
  325.6 18.6 %copy-start.3 = (bf16[512,1,256]{0,2,1:T(8,128)(2,1)S(1)}, bf16[512,1,256]{0,2,1:T(8,128)(2,1)}, u32[]{:S(2)}) copy-start(bf16[512,1,256]{0,2,1:T(8,128)(2,1)} %copy-done.2) | copy-start | bytes 786436
  325.6 90.9 %reduce-scatter.15.cloned.1.call-start = ((), (), s32[]{:S(2)}) async-start(), calls=%async_computation.18 | async-start | bytes 1310720 | tf_op jit(solution)/shard_map/reduce_scatter | solution.py:247
  347.4 3.6 copy-start.21
  347.4 3.6 copy-start.23
  351.0 18.6 %copy-start.17 = (bf16[512,4,32]{0,2,1:T(8,128)(2,1)S(1)}, bf16[512,4,32]{0,2,1:T(8,128)(2,1)}, u32[]{:S(2)}) copy-start(bf16[512,4,32]{0,2,1:T(8,128)(2,1)} %copy-done.16) | copy-start | bytes 393220
  351.0 18.6 %copy-start.19 = (bf16[512,4,32]{0,2,1:T(8,128)(2,1)S(1)}, bf16[512,4,32]{0,2,1:T(8,128)(2,1)}, u32[]{:S(2)}) copy-start(bf16[512,4,32]{0,2,1:T(8,128)(2,1)} %copy-done.18) | copy-start | bytes 393220
  387.9 3.5 copy-start.13
  387.9 3.6 copy-start.8
  391.4 101.6 %reduce-scatter.23.cloned.1.call-start = ((), (), s32[]{:S(2)}) async-start(), calls=%async_computation.22 | async-start | bytes 3022848 | tf_op jit(solution)/shard_map/reduce_scatter | solution.py:219
  393.9 1.2 copy-start.4
  393.9 1.3 copy-start.6
  394.0 2.7 copy-start.14
  394.0 166.0 %reduce-scatter.19.cloned.1.call-start = ((), (), s32[]{:S(2)}) async-start(), calls=%async_computation.20 | async-start | bytes 1179648 | tf_op jit(solution)/shard_map/reduce_scatter | solution.py:259
  396.6 241.5 %reduce-scatter.17.cloned.1.call-start = ((), (), s32[]{:S(2)}) async-start(), calls=%async_computation.19 | async-start | bytes 3538944 | tf_op jit(solution)/shard_map/reduce_scatter | solution.py:258
  400.6 1.1 copy-start.10
  400.6 1.3 copy-start.12
  400.6 345.5 %reduce-scatter.21.cloned.1.call-start = ((), (), s32[]{:S(2)}) async-start(), calls=%async_computation.21 | async-start | bytes 6045696 | tf_op jit(solution)/shard_map/reduce_scatter | solution.py:220
  407.0 9.5 %copy-start.26 = (f32[1024]{0:T(1024)S(1)}, f32[1024]{0:T(1024)}, u32[]{:S(2)}) copy-start(f32[1024]{0:T(1024)} %param.13) | copy-start | bytes 12292
  407.0 9.5 %copy-start.30 = (f32[128]{0:T(128)S(1)}, f32[128]{0:T(128)}, u32[]{:S(2)}) copy-start(f32[128]{0:T(128)} %copy-done.29) | copy-start | bytes 1540
  407.0 9.5 %copy-start.32 = (f32[128]{0:T(128)S(1)}, f32[128]{0:T(128)}, u32[]{:S(2)}) copy-start(f32[128]{0:T(128)} %copy-done.31) | copy-start | bytes 1540
  407.0 10.8 %copy-start.27 = (f32[1024]{0:T(1024)S(1)}, f32[1024]{0:T(1024)}, u32[]{:S(2)}) copy-start(f32[1024]{0:T(1024)} %get-tuple-element.54) | copy-start | bytes 12292
  (3 other events, 2.1 us)
Sparse Core Ops, SparseCore 0:
  12.1 19.4 all-gather.7
  34.2 45.2 all-gather.9
  90.8 29.5 reduce-scatter.8
  121.9 16.7 all-gather.17
  140.8 42.5 all-gather.15
  185.5 56.2 all-gather.13
  244.0 14.8 all-gather.11
  271.2 24.8 reduce-scatter.12
  298.6 24.8 reduce-scatter.10
  325.7 16.7 all-gather.19
  391.6 24.8 reduce-scatter.14
  420.4 72.5 reduce-scatter.22
  497.4 62.5 reduce-scatter.18
  564.0 74.0 reduce-scatter.16
  642.1 103.9 reduce-scatter.20
where the time goes:
time: 753 us
  waiting for transfers between devices  560 us (74%)
  matrix products  78.5 us (10%)
  blocking collectives  69.9 us (9%)
  other arithmetic  21.1 us (3%)
  between operations  14.5 us (2%)
  local copies, waits for them, and re-layouts  7.57 us (1%)
    reduce_scatter x1, waiting for transfers between devices, local(): lax.psum_scatter(expand_term, 'dp', scatter_dimension=0, tiled=True)  108 us
    reduce_scatter x1, waiting for transfers between devices, local(): lax.psum_scatter(merged_term, 'dp', scatter_dimension=0, tiled=True)  78.1 us
    reduce_scatter x1, waiting for transfers between devices, local(): lax.psum_scatter(output_term, 'dp', scatter_dimension=1, tiled=True)  66.9 us
    all_gather x1, waiting for transfers between devices, local(): lax.all_gather(expand_weight, 'dp', axis=0, tiled=True)  55.8 us
    all_gather x1, waiting for transfers between devices, local(): lax.all_gather(shrink_weight, 'dp', axis=1, tiled=True)  44.7 us
    psum x1, blocking collectives, local(): lax.psum((gain_one_term, gain_two_term), ('dp', 'tensor'))  40.4 us
    all_gather x1, waiting for transfers between devices, local(): lax.all_gather(merged_weight, 'dp', axis=0, tiled=True)  36.1 us
    reduce_scatter x1, waiting for transfers between devices, local(): lax.psum_scatter(shrink_term, 'dp', scatter_dimension=1, tiled=True)  32.9 us
  transfers between devices with their start and end apart: 15, of which 14 were waited for; matrix products, arithmetic and copies ran while one was open for 4% of the time, Pallas kernels for 0%

commit v1 on v0

v1 whole, which is shorter than its diff:
```python
from functools import partial

import jax
import jax.numpy as jnp
from jax import lax
from jax.experimental import pallas as pl
from jax.experimental.pallas import tpu as pltpu
from jax.sharding import PartitionSpec as P

WINDOW = 128
HEAD_DIM = 64
MESH = pl.DeviceIdType.MESH

epsilon = 1e-05
rope_base = 10000.0
masked_score = -1e30
BF = jnp.bfloat16
F32 = jnp.float32


def dot(a, b, dims=((1,), (0,))):
    return lax.dot_general(a, b, (dims, ((), ())), preferred_element_type=F32)


def normalize(rows):
    center = rows - jnp.mean(rows, axis=-1, keepdims=True)
    inverse = lax.rsqrt(jnp.mean(center * center, axis=-1, keepdims=True) + epsilon)
    return center * inverse, inverse


def norm_back(grad, hat, inverse, gain):
    gain_term = jnp.sum(grad * hat, axis=0, keepdims=True)
    grad_hat = grad * gain
    mean_grad = jnp.mean(grad_hat, axis=-1, keepdims=True)
    mean_cross = jnp.mean(grad_hat * hat, axis=-1, keepdims=True)
    return (grad_hat - mean_grad - hat * mean_cross) * inverse, gain_term


def swap_halves(rows):
    half = HEAD_DIM // 2
    width = rows.shape[1]
    lane = lax.broadcasted_iota(jnp.int32, rows.shape, 1)
    ahead = pltpu.roll(rows, width - half, 1)
    behind = pltpu.roll(rows, half, 1)
    return jnp.where(lane % HEAD_DIM < half, ahead, behind)


def key_start(block, rows, group, wide):
    return max(0, min(block * rows - WINDOW // 2, group - wide))


def band_probs(q, k, seg_q, seg_k, q_at, k_at):
    raw = dot(q, k, ((1,), (1,))) * HEAD_DIM ** (-0.5)
    row = q_at + lax.broadcasted_iota(jnp.int32, raw.shape, 0)
    col = k_at + lax.broadcasted_iota(jnp.int32, raw.shape, 1)
    ok = (seg_q == seg_k) & (jnp.abs(row - col) <= WINDOW // 2)
    score = jnp.where(ok, raw, masked_score)
    weight = jnp.exp(score - jnp.max(score, axis=-1, keepdims=True))
    return weight / jnp.sum(weight, axis=-1, keepdims=True)


class Place:
    def __init__(self, dp, tn):
        self.dp, self.tn = dp, tn
        self.d, self.t = lax.axis_index("dp"), lax.axis_index("tensor")
        self.outer = dp // 2
        self.o, self.i = self.d // 2, self.d % 2
        self.x, self.c = self.t // 2, self.t % 2
        self.core = (self.d, self.x * 2 + 1 - self.c)
        self.across = (self.d, (1 - self.x) * 2 + self.c)
        self.y = (self.o * 2 + 1 - self.i, self.t)

    def ahead(self, s):
        return (self.o + s) % self.outer

    def back(self, s):
        return (self.o + self.outer - s) % self.outer

    def z(self, s):
        return (self.ahead(s) * 2 + self.i, self.t)

    def barrier(self):
        sem = pltpu.get_barrier_semaphore()
        peers = [self.core, self.across, self.y]
        peers += [self.z(s) for s in range(1, self.outer)]
        for peer in peers:
            pl.semaphore_signal(sem, inc=1, device_id=peer, device_id_type=MESH)
        pl.semaphore_wait(sem, len(peers))


def send(src, dst, sems, index, peer):
    copy = pltpu.make_async_remote_copy(
        src_ref=src,
        dst_ref=dst,
        send_sem=sems.at[0, index],
        recv_sem=sems.at[1, index],
        device_id=peer,
        device_id_type=MESH,
    )
    copy.start()
    return copy


class TensorGather:
    def __init__(self, place, full, sems, base):
        p = self.p = place
        self.full, self.sems, self.base = full, sems, base
        self.first = send(full.at[p.t], full.at[p.t], sems, base, p.across)
        self.second = send(full.at[p.t], full.at[p.t], sems, base + 1, p.core)

    def forward(self):
        p = self.p
        self.first.wait_recv()
        at = p.across[1]
        self.third = send(self.full.at[at], self.full.at[at], self.sems, self.base + 2, p.core)

    def finish(self):
        self.second.wait_recv()
        self.third.wait_recv()
        for copy in (self.first, self.second, self.third):
            copy.wait_send()


class TensorScatter:
    def __init__(self, place, part, cbuf, held, xbuf, sems, base):
        p = self.p = place
        self.part, self.cbuf, self.held, self.xbuf = part, cbuf, held, xbuf
        self.sems, self.base = sems, base
        self.far = send(part.at[(1 - p.x) * 2 + 1 - p.c], cbuf.at[0], sems, base, p.core)
        self.near = send(part.at[p.x * 2 + 1 - p.c], cbuf.at[1], sems, base + 1, p.core)

    def forward(self):
        p = self.p
        self.far.wait_recv()
        both = self.part[(1 - p.x) * 2 + p.c].astype(F32) + self.cbuf[0].astype(F32)
        self.held[...] = both.astype(BF)
        self.last = send(self.held, self.xbuf, self.sems, self.base + 2, p.across)

    def finish(self):
        self.near.wait_recv()
        own = self.part[self.p.t].astype(F32) + self.cbuf[1].astype(F32)
        self.last.wait_recv()
        total = own + self.xbuf[...].astype(F32)
        for copy in (self.far, self.near, self.last):
            copy.wait_send()
        return total


def block_of(ref, at):
    return ref.at[:, at] if len(ref.shape) == 4 else ref.at[at]


class WeightGather:
    def __init__(self, place, shard, full, zsem, ysem, lsem):
        p = self.p = place
        self.full, self.ysem = full, ysem
        own = block_of(full, p.d)
        self.zs = [send(shard, own, zsem, s - 1, p.z(s)) for s in range(1, p.outer)]
        self.ys = [send(shard, own, ysem, 0, p.y)]
        self.local = pltpu.make_async_copy(shard, own, lsem)
        self.local.start()

    def forward(self):
        p = self.p
        for s in range(1, p.outer):
            self.zs[s - 1].wait_recv()
            at = block_of(self.full, p.back(s) * 2 + p.i)
            self.ys.append(send(at, at, self.ysem, s, p.y))

    def finish(self):
        self.local.wait()
        for copy in self.ys:
            copy.wait_recv()

    def sent(self):
        for copy in self.zs + self.ys:
            copy.wait_send()


class GradScatter:
    def __init__(self, place, grads, ybuf, ysum, zbuf, zsem, ysem):
        p = self.p = place
        self.grads, self.ybuf, self.ysum, self.zbuf, self.zsem = grads, ybuf, ysum, zbuf, zsem
        self.ys = {}
        for s in self.order():
            block = block_of(grads, p.ahead(s) * 2 + 1 - p.i)
            self.ys[s] = send(block, ybuf.at[s], ysem, s, p.y)
        self.zs = []

    def order(self):
        return list(range(1, self.p.outer)) + [0]

    def pair(self, s):
        self.ys[s].wait_recv()
        own = block_of(self.grads, self.p.ahead(s) * 2 + self.p.i)
        return own[...].astype(F32) + self.ybuf[s].astype(F32)

    def forward(self):
        p = self.p
        for s in range(1, p.outer):
            self.ysum[s - 1] = self.pair(s).astype(BF)
            self.zs.append(send(self.ysum.at[s - 1], self.zbuf.at[s - 1], self.zsem, s - 1, p.z(s)))

    def finish(self):
        total = self.pair(0)
        for s in range(1, self.p.outer):
            self.zs[s - 1].wait_recv()
            total = total + self.zbuf[s - 1].astype(F32)
        for copy in self.zs + list(self.ys.values()):
            copy.wait_send()
        return total


def first_kernel(dp, tn, x, g1, g2, cot, cs, sn, segc, segr, wa, we, ws,
                 fa, fe, fs, n1, n2, cotg, q_out, k_out, v_out, att, mid,
                 part, cbuf, held, xbuf, tsem, az, ay, ez, ey, sz, sy, lsem):
    p = Place(dp, tn)
    p.barrier()
    ga = WeightGather(p, wa, fa, az, ay, lsem.at[0])
    rows = x[...].astype(F32)
    hat, unused = normalize(rows)
    n1[p.t] = (hat * g1[...]).astype(BF)
    cotg[p.t] = cot[...]
    gn = TensorGather(p, n1, tsem, 0)
    ge = WeightGather(p, we, fe, ez, ey, lsem.at[1])
    gs = WeightGather(p, ws, fs, sz, sy, lsem.at[2])
    gn.forward()
    ga.forward()
    gn.finish()
    ga.finish()
    group = n1.shape[0] * n1.shape[1]
    width = q_out.shape[1]
    depth = fa.shape[0] * fa.shape[1]
    tokens = n1[...].reshape(group, depth)
    merged = dot(tokens, fa[:, :, : 3 * width].reshape(depth, 3 * width))
    for ref, at in ((q_out, 0), (k_out, 1)):
        piece = merged[:, at * width : (at + 1) * width]
        ref[...] = (piece * cs[...] + swap_halves(piece) * sn[...]).astype(BF)
    v_out[...] = merged[:, 2 * width :].astype(BF)
    gc = TensorGather(p, cotg, tsem, 3)
    size = min(128, group)
    wide = min(size + WINDOW, group)
    for h in range(width // HEAD_DIM):
        cols = slice(h * HEAD_DIM, (h + 1) * HEAD_DIM)
        for b in range(group // size):
            lo = key_start(b, size, group, wide)
            qr, kr = slice(b * size, (b + 1) * size), slice(lo, lo + wide)
            probs = band_probs(q_out[qr, cols], k_out[kr, cols], segc[qr], segr[:, kr], b * size, lo)
            att[qr, cols] = dot(probs.astype(BF), v_out[kr, cols]).astype(BF)
    out_t = fa[:, :, 3 * width :].reshape(depth, width)
    part[...] = dot(att[...], out_t, ((1,), (1,))).astype(BF).reshape(part.shape)
    rs = TensorScatter(p, part, cbuf, held, xbuf, tsem, 6)
    gc.forward()
    rs.forward()
    ge.forward()
    middle = rows + rs.finish()
    mid[...] = middle
    hat_two, unused = normalize(middle)
    n2[p.t] = (hat_two * g2[...]).astype(BF)
    gm = TensorGather(p, n2, tsem, 9)
    gs.forward()
    gm.forward()
    gm.finish()
    gc.finish()
    ge.finish()
    gs.finish()
    for gather in (ga, ge, gs):
        gather.sent()


def second_kernel(dp, tn, pm, pd, mid, cot, x, g1, g2, cs, sn, segc, segr, fa, n1, q_in, k_in, v_in,
                  att, gre, grs,
                  out, din, oa, oe, os_, gains,
                  gra, branch, part, cbuf, held, xbuf, dqkv, dat,
                  ya, sa, za, ye, se, ze, ys, ss, zs, tbuf, ybuf, zbuf, tsem,
                  az, ay, ez, ey, sz, sy, gsem):
    p = Place(dp, tn)
    p.barrier()
    rd = TensorScatter(p, pd, cbuf.at[0], held.at[0], xbuf.at[0], tsem, 0)
    rm = TensorScatter(p, pm, cbuf.at[1], held.at[1], xbuf.at[1], tsem, 3)
    se_ = [GradScatter(p, grs, ys, ss, zs, sz, sy), GradScatter(p, gre, ye, se, ze, ez, ey)]
    rd.forward()
    rm.forward()
    middle = mid[...]
    hat_two, inv_two = normalize(middle)
    back, gain_two = norm_back(rd.finish(), hat_two, inv_two, g2[...])
    dmid = cot[...].astype(F32) + back
    branch[p.t] = dmid.astype(BF)
    gb = TensorGather(p, branch, tsem, 6)
    out[...] = (middle + rm.finish()).astype(BF)
    gb.forward()
    gb.finish()
    group = n1.shape[0] * n1.shape[1]
    width = q_in.shape[1]
    depth = fa.shape[0] * fa.shape[1]
    da = branch[...].reshape(group, depth)
    dat[...] = dot(da, fa[:, :, 3 * width :].reshape(depth, width)).astype(BF)
    gra[:, :, 3 * width :] = dot(da, att[...], ((0,), (0,))).astype(BF).reshape(
        gra.shape[0], gra.shape[1], width)
    dqkv[:, width:] = jnp.zeros((group, 2 * width), F32)
    size = min(128, group)
    wide = min(size + WINDOW, group)
    for h in range(width // HEAD_DIM):
        qc, kc, vc = (slice(n * width + h * HEAD_DIM, n * width + (h + 1) * HEAD_DIM) for n in range(3))
        for b in range(group // size):
            lo = key_start(b, size, group, wide)
            qr, kr = slice(b * size, (b + 1) * size), slice(lo, lo + wide)
            q, k, v, g = q_in[qr, qc], k_in[kr, qc], v_in[kr, qc], dat[qr, qc]
            probs = band_probs(q, k, segc[qr], segr[:, kr], b * size, lo)
            dqkv[kr, vc] += dot(probs.astype(BF), g, ((0,), (0,)))
            dprobs = dot(g, v, ((1,), (1,)))
            inner = jnp.sum(dprobs * probs, axis=-1, keepdims=True)
            draw = (probs * (dprobs - inner) * HEAD_DIM ** (-0.5)).astype(BF)
            dqkv[qr, qc] = dot(draw, k)
            dqkv[kr, kc] += dot(draw, q, ((0,), (0,)))
    turned = []
    for at in range(2):
        piece = dqkv[:, at * width : (at + 1) * width]
        turned.append((piece * cs[...] - swap_halves(piece) * sn[...]).astype(BF))
    turned.append(dqkv[:, 2 * width :].astype(BF))
    fused = jnp.concatenate(turned, axis=1)
    part[...] = dot(fused, fa[:, :, : 3 * width].reshape(depth, 3 * width), ((1,), (1,))).astype(BF).reshape(part.shape)
    rn = TensorScatter(p, part, cbuf.at[2], held.at[2], xbuf.at[2], tsem, 9)
    tokens = n1[...].reshape(group, depth)
    gra[:, :, : 3 * width] = dot(tokens, fused, ((0,), (0,))).astype(BF).reshape(
        gra.shape[0], gra.shape[1], 3 * width)
    sca = GradScatter(p, gra, ya, sa, za, az, ay)
    for scatter in se_:
        scatter.forward()
    rn.forward()
    hat, inv = normalize(x[...].astype(F32))
    back, gain_one = norm_back(rn.finish(), hat, inv, g1[...])
    din[...] = dmid + back
    lines = lax.broadcasted_iota(jnp.int32, tbuf.shape[1:], 0)
    tbuf[p.t] = jnp.where(lines == 0, gain_one, jnp.where(lines == 1, gain_two, 0.0))
    gt = TensorGather(p, tbuf, tsem, 12)
    gt.forward()
    sca.forward()
    gt.finish()
    ybuf[p.i] = sum(tbuf[n] for n in range(tn))
    cy = send(ybuf.at[p.i], ybuf.at[p.i], gsem, 0, p.y)
    cy.wait_recv()
    zbuf[p.o] = ybuf[0] + ybuf[1]
    cz = [send(zbuf.at[p.o], zbuf.at[p.o], gsem, s, p.z(s)) for s in range(1, p.outer)]
    os_[...] = se_[0].finish()
    oe[...] = se_[1].finish()
    oa[...] = sca.finish()
    for copy in cz:
        copy.wait_recv()
    gains[...] = sum(zbuf[n] for n in range(p.outer))
    for copy in [cy] + cz:
        copy.wait_send()


def call(kernel, outs, scratch, number, args):
    vmem = pl.BlockSpec(memory_space=pltpu.VMEM)
    return pl.pallas_call(
        kernel,
        out_shape=outs,
        in_specs=[vmem] * len(args),
        out_specs=[vmem] * len(outs),
        scratch_shapes=scratch,
        compiler_params=pltpu.CompilerParams(
            collective_id=number, has_side_effects=True, vmem_limit_bytes=56 << 20
        ),
    )(*args)


def local(dp, tn, layer_input, segments, positions, first_gain, merged_weight, output_weight,
          second_gain, expand_weight, shrink_weight, cotangent):
    rows, unused, width = merged_weight.shape
    units = expand_weight.shape[2]
    here, depth = layer_input.shape
    group = segments.shape[0]
    outer = dp // 2
    half = HEAD_DIM // 2
    sds = jax.ShapeDtypeStruct
    frequency = rope_base ** (-2.0 * jnp.arange(half, dtype=F32) / HEAD_DIM)
    angles = positions.astype(F32)[:, None] * frequency[None, :]
    cosine, sine = jnp.cos(angles), jnp.sin(angles)
    cs = jnp.tile(jnp.concatenate([cosine, cosine], axis=1), (1, width // HEAD_DIM))
    sn = jnp.tile(jnp.concatenate([-sine, sine], axis=1), (1, width // HEAD_DIM))
    segc, segr = segments[:, None], segments[None, :]
    g1, g2 = first_gain[None], second_gain[None]
    wa = jnp.concatenate([merged_weight.reshape(rows, 3 * width), output_weight.T], axis=1)
    we = expand_weight.transpose(1, 0, 2)
    ws = shrink_weight.T
    side = wa.shape[1]
    dma = pltpu.SemaphoreType.DMA
    zsem, ysem = dma((2, outer - 1)), dma((2, outer))
    slab = (tn, here, depth)
    fa, fe, fs, n1, n2, cotg, q, k, v, att, mid = call(
        partial(first_kernel, dp, tn),
        [sds((dp, rows, side), BF), sds((2, dp, rows, units), BF), sds((dp, rows, units), BF),
         sds(slab, BF), sds(slab, BF), sds(slab, BF)]
        + [sds((group, width), BF)] * 4 + [sds((here, depth), F32)],
        [pltpu.VMEM(slab, BF), pltpu.VMEM((2, here, depth), BF), pltpu.VMEM((here, depth), BF),
         pltpu.VMEM((here, depth), BF), dma((2, 12)), zsem, ysem, zsem, ysem, zsem, ysem, dma((3,))],
        0, (layer_input, g1, g2, cotangent, cs, sn, segc, segr, wa, we, ws))

    tokens = n2.reshape(group, depth)
    grad_mlp = cotg.reshape(group, depth)
    expand = fe.reshape(2, depth, units)
    shrink_t = fs.reshape(depth, units)
    gate, up = dot(tokens, expand[0]), dot(tokens, expand[1])
    activated, gelu_back = jax.vjp(partial(jax.nn.gelu, approximate=False), gate)
    hidden = (activated * up).astype(BF)
    pm = dot(hidden, shrink_t, ((1,), (1,))).astype(BF).reshape(slab)
    grad_hidden = dot(grad_mlp, shrink_t)
    d_in = gelu_back(grad_hidden * up)[0].astype(BF)
    d_gate = (grad_hidden * activated).astype(BF)
    pd = (dot(d_in, expand[0], ((1,), (1,))) + dot(d_gate, expand[1], ((1,), (1,)))).astype(BF).reshape(slab)
    grs = dot(grad_mlp, hidden, ((0,), (0,))).astype(BF).reshape(dp, rows, units)
    gre = jnp.stack([dot(tokens, d_in, ((0,), (0,))).astype(BF), dot(tokens, d_gate, ((0,), (0,))).astype(BF)])
    gre = gre.reshape(2, dp, rows, units)

    def bufs(shape):
        return [pltpu.VMEM((outer,) + shape, BF)] + [pltpu.VMEM((outer - 1,) + shape, BF)] * 2

    out, din, oa, oe, os_, gains = call(
        partial(second_kernel, dp, tn),
        [sds((here, depth), BF), sds((here, depth), F32), sds((rows, side), F32),
         sds((2, rows, units), F32), sds((rows, units), F32), sds((8, depth), F32)],
        [pltpu.VMEM((dp, rows, side), BF), pltpu.VMEM(slab, BF), pltpu.VMEM(slab, BF),
         pltpu.VMEM((3, 2, here, depth), BF), pltpu.VMEM((3, here, depth), BF),
         pltpu.VMEM((3, here, depth), BF), pltpu.VMEM((group, 3 * width), F32),
         pltpu.VMEM((group, width), BF)]
        + bufs((rows, side)) + bufs((2, rows, units)) + bufs((rows, units))
        + [pltpu.VMEM((tn, 8, depth), F32), pltpu.VMEM((2, 8, depth), F32),
           pltpu.VMEM((outer, 8, depth), F32), dma((2, 15)),
           zsem, ysem, zsem, ysem, zsem, ysem, ysem],
        1, (pm, pd, mid, cotangent, layer_input, g1, g2, cs, sn, segc, segr, fa, n1, q, k, v, att, gre, grs))
    return (out, din, gains[0], oa[:, : 3 * width].reshape(rows, 3, width), oa[:, 3 * width :].T,
            gains[1], oe.transpose(1, 0, 2), os_.T)


def solution(mesh):
    placed = (
        P(("dp", "tensor"), None), P("dp"), P("dp"), P(), P("dp", None, "tensor"), P("tensor", "dp"),
        P(), P("dp", None, "tensor"), P("tensor", "dp"), P(("dp", "tensor"), None),
    )
    return jax.shard_map(
        partial(local, mesh.shape["dp"], mesh.shape["tensor"]),
        mesh=mesh,
        in_specs=placed,
        out_specs=(
            P(("dp", "tensor"), None), P(("dp", "tensor"), None), P(), P("dp", None, "tensor"),
            P("tensor", "dp"), P(), P("dp", None, "tensor"), P("tensor", "dp"),
        ),
        check_vma=False,
    )
```

time: 753 us -> 277 us (0.37)
  waiting for transfers between devices: 560 us -> 0 us
  Pallas kernels: 0 us -> 230 us
  blocking collectives: 69.9 us -> 0 us
  matrix products: 78.5 us -> 18.8 us
  other arithmetic: 21.1 us -> 3.76 us
  local copies, waits for them, and re-layouts: 7.57 us -> 23.7 us
  between operations: 14.5 us -> 0.86 us
    reduce_scatter x8 -> x0, waiting for transfers between devices: 372 us -> none  [the longest x1 108 us: local(): lax.psum_scatter(expand_term, 'dp', scatter_dimension=0, tiled=True)]
    pallas_call x0 -> x2, Pallas kernels: none -> 230 us  [call(): pl.pallas_call(kernel, out_shape=outs, in_specs=[vmem] * len(args), out_s...]
    all_gather x7 -> x0, waiting for transfers between devices: 186 us -> none  [the longest x1 55.8 us: local(): lax.all_gather(expand_weight, 'dp', axis=0, tiled=True)]
    dot_general x18 -> x9, matrix products: 78.5 us -> 18.8 us  [dot(): return lax.dot_general(a, b, (dims, ((), ())), preferred_element_type=F32)]
    psum x1 -> x0, blocking collectives: 40.4 us -> none  [local(): lax.psum((gain_one_term, gain_two_term), ('dp', 'tensor'))]
    all_gather x1 -> x0, blocking collectives: 29.5 us -> none  [local(): lax.all_gather(output_weight, 'dp', axis=1, tiled=True)]
    reduce_sum x7 -> x0, other arithmetic: 8.02 us -> none  [the longest x2 3.06 us: norm_back(): gain_term = jnp.sum(grad_normed * normal_rows, axis=0)]
  transfers between devices with their start and end apart: 15 -> 0, of which waited for: 14 -> 0; matrix products, arithmetic and copies ran while one was open for 4% -> 0% of each run, Pallas kernels for 0% -> 0%
where the time goes in v1:
time: 277 us
  Pallas kernels  230 us (83%)
  local copies, waits for them, and re-layouts  23.7 us (9%)
  matrix products  18.8 us (7%)
  other arithmetic  3.76 us (1%)
    pallas_call x2, Pallas kernels, call(): pl.pallas_call(kernel, out_shape=outs, in_specs=[vmem] * len(args), out_s...  230 us
    dot_general x9, matrix products, dot(): return lax.dot_general(a, b, (dims, ((), ())), preferred_element_type=F32)  18.8 us
    unnamed x36, local copies, waits for them, and re-layouts  9.76 us

profile of v1, /device:TPU:0, one launch (start us, length us, event | category | flops | bytes accessed | tf_op | source)
XLA Modules:
  0.0 276.8 jit_solution(1029788528645005733)
XLA Ops:
  0.6 0.0 copy-start.6
  0.6 0.0 copy-start.5
  0.7 0.7 convert_element_type.27
  1.4 0.9 copy.30
  2.3 0.3 fusion.6
  2.7 1.1 copy.29
  3.8 0.2 copy.31
  3.9 0.0 copy-start.3
  4.0 0.7 pad_maximum_fusion.1.wa
  4.7 0.0 copy-done.5
  4.7 0.8 copy.33
  5.5 0.9 copy.36.segc
  6.4 0.1 tile.8
  6.4 1.0 copy.34.cs
  7.4 0.0 copy-done.3
  7.4 0.9 copy.32
  8.4 1.0 copy.35.sn
  9.4 102.3 %shard_map.161 = (bf16[8,128,1024]{2,1,0:T(8,128)(2,1)}, bf16[2,8,128,656]{3,2,1,0:T(8,128)(2,1)}, bf16[8,128,656]{2,1,0:T(8,128)(2,1)}, bf16[4,128,1024]{2,1,0:...) custom-call(bf16[128,1024]{1,0:T(8,128)(2,1)} %x.3, ...), custom_call_target="tpu_custom_call" | custom-call | tf_op jit(solution)/shard_map/pallas_call | solution.py:357
  111.7 2.2 fusion.8
  113.9 0.9 fusion.10
  114.9 0.5 copy-done.7
  115.3 0.3 copy-done.10
  115.6 4.5 %multiply_convert_fusion = (bf16[512,656]{0,1:T(8,128)(2,1)}, f32[512,656]{0,1:T(8,128)S(1)}, f32[512,656]{0,1:T(8,128)S(1)}) fusion(f32[512,656]{0,1:T(8,128)S(1)} %fusion.10, bf16[512,1024]{1,0:T(8,128)(2,1)S(1)} %bitcast.78, bf16[1024,656]{1,0:T(8,128)(2,1)S(1)} %bitcast.72), kind=kOutput, calls=%fused_computation.8 | convolution fusion | flops 710033408 | bytes 7094272 | tf_op jit(solution)/shard_map/dot_general | solution.py:22
  120.1 2.3 add_convert_fusion.1
  122.4 2.1 convolution_convert_fusion.3
  124.5 1.9 convolution_convert_fusion
  126.5 2.5 copy.39
  129.0 2.2 fusion.11
  131.2 2.0 add_convert_fusion
  133.2 1.9 convolution_convert_fusion.1
  135.2 0.0 copy-done.12
  135.2 0.9 convolution_convert_fusion.2
  136.1 0.7 copy.37
  136.8 1.9 copy.38
  138.7 2.0 pad_maximum_fusion.gre
  140.6 127.3 %shard_map.162 = (bf16[128,1024]{1,0:T(8,128)(2,1)}, f32[128,1024]{1,0:T(8,128)}, f32[128,1024]{1,0:T(8,128)}, f32[2,128,656]{2,1,0:T(8,128)}, f32[128,656]{1,0:T(8,128)}, /*index=5*/f32[8,1024]{1,0:T(8,128)}) custom-call(bf16[4,128,1024]{2,1,0:T(8,128)(2,1)} %bitcast.56, bf16[4,128,1024]{2,1,0:T(8,128)(2,1)} %bitcast.57, ...), custom_call_target="tpu_custom_call" | custom-call | tf_op jit(solution)/shard_map/pallas_call | solution.py:357
  268.0 1.4 fusion.9
  269.4 0.9 slice_bitcast_fusion
  270.3 1.1 slice.25
  271.4 0.2 copy.43
  271.6 0.9 copy.44
  272.5 0.8 copy.45
  273.3 0.9 copy.47
  274.1 0.0 copy-done
  274.1 1.1 copy.46
  275.3 0.0 copy-done.4
  275.3 0.7 copy.50
  276.0 0.8 copy.51
  (19 shorter events, 0.1 us)
Async XLA Ops:
  0.6 4.9 %copy-start.6 = (s32[512]{0:T(512)S(1)}, s32[512]{0:T(512)}, u32[]{:S(2)}) copy-start(s32[512]{0:T(512)} %param.11) | copy-start | bytes 6148
  0.6 4.0 %copy-start.5 = (bf16[656,128]{1,0:T(8,128)(2,1)S(1)}, bf16[656,128]{1,0:T(8,128)(2,1)}, u32[]{:S(2)}) copy-start(bf16[656,128]{1,0:T(8,128)(2,1)} %param.18) | copy-start | bytes 503812
  3.9 3.5 %copy-start.3 = (bf16[128,2,656]{0,2,1:T(8,128)(2,1)S(1)}, bf16[128,2,656]{0,2,1:T(8,128)(2,1)}, u32[]{:S(2)}) copy-start(bf16[128,2,656]{0,2,1:T(8,128)(2,1)} %param.17) | copy-start | bytes 1007620
  111.7 2.2 copy-start.8
  113.9 1.4 copy-start.7
  113.9 1.7 copy-start.10
  129.0 2.2 copy-start.11
  131.2 2.0 copy-start.9
  133.2 2.0 copy-start.12
  270.3 2.9 %copy-start.2 = (f32[128,656]{1,0:T(8,128)S(1)}, f32[128,656]{1,0:T(8,128)}, u32[]{:S(2)}) copy-start(f32[128,656]{1,0:T(8,128)} %get-tuple-element.41) | copy-start | bytes 1007620
  271.4 2.8 copy-start
  272.5 2.8 %copy-start.4 = (bf16[128,1024]{1,0:T(8,128)(2,1)S(1)}, bf16[128,1024]{1,0:T(8,128)(2,1)}, u32[]{:S(2)}) copy-start(bf16[128,1024]{1,0:T(8,128)(2,1)} %get-tuple-element.80) | copy-start | bytes 786436
  273.2 2.7 copy-start.1
